TPU v7x, 32 devices: a whole 2x2x4 slice. The times are simulated.
32 devices in a mesh: dp: 8 (over z, x), feat: 4 (over y, core).
Axes of the slice: x: 2, y: 2, z: 4, core: 2. Of those that a mesh axis runs over, the one named last changes fastest.
Arguments:
- tokens: bfloat16 [4096, 1024], P('dp'), may hold values from -6 to 6
- gain_one: float32 [1024], replicated, may hold values from 0.5 to 1.5
- w_query: bfloat16 [1024, 256], replicated, may hold values from -0.1875 to 0.1875
- w_key: bfloat16 [1024, 256], replicated, may hold values from -0.1875 to 0.1875
- w_value: bfloat16 [1024, 1024], replicated, may hold values from -0.1875 to 0.1875
- w_out: bfloat16 [1024, 1024], replicated, may hold values from -1.5 to 1.5
- gain_two: float32 [1024], replicated, may hold values from 0.5 to 1.5
- w_gate: bfloat16 [1024, 2752], P(None, 'feat'), may hold values from -0.1875 to 0.1875
- w_up: bfloat16 [1024, 2752], P(None, 'feat'), may hold values from -0.1875 to 0.1875
- w_down: bfloat16 [2752, 1024], P('feat'), may hold values from -0.109375 to 0.109375
- lengths: int32 [8, 4], P('dp'), may hold values from 0 to 512, as said below
- cotangent: bfloat16 [4096, 1024], P('dp'), may hold values from -6 to 6
Outputs:
- output: bfloat16 [4096, 1024], P('dp')
- grad_input: bfloat16 [4096, 1024], P('dp')
- grad_gain_one: float32 [1024], P('dp')
- grad_w_query: float32 [1024, 256], P('dp')
- grad_w_key: float32 [1024, 256], P('dp')
- grad_w_value: float32 [1024, 1024], P('dp')
- grad_w_out: float32 [1024, 1024], P('feat', 'dp')
- grad_gain_two: float32 [1024], P('dp')
- grad_w_gate: float32 [1024, 2752], P('dp', 'feat')
- grad_w_up: float32 [1024, 2752], P('dp', 'feat')
- grad_w_down: float32 [2752, 1024], P('feat', 'dp')
Inputs may be any that keep to these rules, and one draw needn't show every extreme that they name: `lengths`: row p lists the sequences packed from slot 0 of dp position p, in order; a row sums to at most 512, zeros are empty slots, and the slots after the sum are padding. One dp position holds a single sequence of 512 tokens.
All inputs are finite; a program needn't handle non-finite values.
Results may differ from a plain program's by a relative error of at most 0.023.
Values may be sent and summed in bfloat16 or wider, within the bound.
No kernel may reach another device: no remote copies, remote signals or barrier semaphores. Data moves between devices by JAX's collectives and lax.ppermute only.
A program may use at most 192 MiB of HBM per device.

v0:
```python
import math
import jax
import jax.numpy as jnp
from jax import lax
from jax.sharding import PartitionSpec as P

HEADS = 16
QK = 16
VD = 64
BLOCK = 512
EPSILON = 1e-05


def rms_factor(values):
    return lax.rsqrt(jnp.mean(values * values, axis=-1, keepdims=True) + EPSILON)


def norm_back(values, factor, gain_row, incoming):
    weighted = incoming * gain_row
    gain_grad = jnp.sum(incoming * values * factor, axis=0)
    value_grad = factor * weighted - values * factor * factor * factor * jnp.mean(
        weighted * values, axis=-1, keepdims=True
    )
    return (gain_grad, value_grad)


def split_parts(array):
    if array.dtype == jnp.bfloat16:
        return (array,)
    leading = array.astype(jnp.bfloat16)
    remainder = (array - leading.astype(jnp.float32)).astype(jnp.bfloat16)
    return (leading, remainder)


def exact_einsum(form, first, second):
    first_parts = split_parts(first)
    second_parts = split_parts(second)
    total = None
    for left_rank, left_part in enumerate(first_parts):
        for right_rank, right_part in enumerate(second_parts):
            if left_rank + right_rank < 2:
                term = jnp.einsum(form, left_part, right_part, preferred_element_type=jnp.float32)
                total = term if total is None else total + term
    return total


def feature_slice(projected, first_feature, slice_width, padded):
    row_count = projected.shape[0]
    split_heads = projected.reshape(row_count, -1, QK)
    heads_count = split_heads.shape[1]
    ones_part = jnp.ones((row_count, heads_count, 1), jnp.float32)
    linear = split_heads * QK ** (-0.25)
    square = (split_heads[:, :, :, None] * split_heads[:, :, None, :]).reshape(
        row_count, heads_count, QK * QK
    ) / math.sqrt(2.0 * QK)
    zeros_part = jnp.zeros((row_count, heads_count, padded - 1 - QK - QK * QK), jnp.float32)
    whole_map = jnp.concatenate([ones_part, linear, square, zeros_part], axis=2)
    return lax.dynamic_slice_in_dim(whole_map, first_feature, slice_width, 2)


def block_allowed(seg_block):
    places = jnp.arange(seg_block.shape[0], dtype=jnp.int32)
    return (places[:, None] >= places[None, :]) & (seg_block[:, None] == seg_block[None, :])


def segment_states(key_side, value_side, extra_side, seg_blocks, reverse):
    heads_count = key_side.shape[2]
    feature_count = key_side.shape[3]
    column_count = value_side.shape[3]

    def advance(carry_data, block_data):
        carried_state, carried_total, marker = carry_data
        key_block, value_block, extra_block, seg_block = block_data
        edge_segment = seg_block[0] if reverse else seg_block[-1]
        keep_state = (edge_segment == marker).astype(jnp.float32)
        chosen = seg_block == edge_segment
        key_selected = jnp.where(chosen[:, None, None], key_block, jnp.zeros_like(key_block))
        state_next = keep_state * carried_state + exact_einsum(
            "jhf,jhc->hfc", key_selected, value_block
        )
        total_next = keep_state * carried_total + exact_einsum(
            "jhf,jh->hf", key_selected, extra_block
        )
        return ((state_next, total_next, edge_segment), (carried_state, carried_total, marker))

    initial = (
        jnp.zeros((heads_count, feature_count, column_count), jnp.float32),
        jnp.zeros((heads_count, feature_count), jnp.float32),
        jnp.int32(-1),
    )
    _, entering = lax.scan(
        advance, initial, (key_side, value_side, extra_side, seg_blocks), reverse=reverse
    )
    return entering


def forward_block(inputs):
    query_block, key_block, value_block, seg_block, carried_state, carried_total, marker = inputs
    allowed = block_allowed(seg_block)
    scores = jnp.einsum("ihf,jhf->hij", query_block, key_block, preferred_element_type=jnp.float32)
    scores = jnp.where(allowed[None], scores, 0.0)
    numerator = exact_einsum("hij,jhc->ihc", scores, value_block)
    denominator = jnp.sum(scores, axis=2).T
    carried = (seg_block == marker).astype(jnp.float32)
    numerator = numerator + carried[:, None, None] * exact_einsum(
        "ihf,hfc->ihc", query_block, carried_state
    )
    denominator = denominator + carried[:, None] * exact_einsum(
        "ihf,hf->ih", query_block, carried_total
    )
    return (numerator, denominator)


def backward_block(inputs):
    (
        query_block,
        key_block,
        value_block,
        seg_block,
        grad_numer,
        grad_denom,
        carried_state,
        carried_total,
        marker,
        later_state,
        later_total,
        later_marker,
    ) = inputs
    allowed = block_allowed(seg_block)
    scores = jnp.einsum("ihf,jhf->hij", query_block, key_block, preferred_element_type=jnp.float32)
    scores = jnp.where(allowed[None], scores, 0.0)
    grad_scores = exact_einsum("ihc,jhc->hij", grad_numer, value_block) + grad_denom.T[:, :, None]
    grad_scores = jnp.where(allowed[None], grad_scores, 0.0)
    grad_query = exact_einsum("hij,jhf->ihf", grad_scores, key_block)
    grad_key = exact_einsum("hij,ihf->jhf", grad_scores, query_block)
    grad_value = exact_einsum("hij,ihc->jhc", scores, grad_numer)
    forward_on = (seg_block == marker).astype(jnp.float32)[:, None, None]
    grad_query = grad_query + forward_on * (
        exact_einsum("ihc,hfc->ihf", grad_numer, carried_state)
        + grad_denom[:, :, None] * carried_total[None]
    )
    later_on = (seg_block == later_marker).astype(jnp.float32)[:, None, None]
    grad_key = grad_key + later_on * (
        exact_einsum("jhc,hfc->jhf", value_block, later_state) + later_total[None]
    )
    grad_value = grad_value + later_on * exact_einsum("jhf,hfc->jhc", key_block, later_state)
    return (grad_query, grad_key, grad_value)


def local(
    tokens,
    gain_one,
    w_query,
    w_key,
    w_value,
    w_out,
    gain_two,
    w_gate,
    w_up,
    w_down,
    lengths,
    cotangent,
):
    token_count = tokens.shape[0]
    feat_count = lax.axis_size("feat")
    feat_index = lax.axis_index("feat")
    padded = (1 + QK + QK * QK + feat_count - 1) // feat_count * feat_count
    slice_width = padded // feat_count
    head_share = HEADS // feat_count
    column_share = head_share * VD
    block_count = token_count // BLOCK
    places = jnp.arange(token_count, dtype=jnp.int32)
    slots = jnp.arange(lengths.shape[1])
    bounds = jnp.sum(jnp.where(slots[None, :] <= slots[:, None], lengths[0][None, :], 0), axis=1)
    segments = jnp.sum((places[:, None] >= bounds[None, :]).astype(jnp.int32), axis=1)
    live_rows = (places < bounds[-1]).astype(jnp.float32)[:, None]

    def blocked(array):
        return array.reshape((block_count, BLOCK) + array.shape[1:])

    first_feature = feat_index * slice_width

    def make_features(projected):
        return feature_slice(projected, first_feature, slice_width, padded)

    inputs = tokens.astype(jnp.float32)
    scale_one = rms_factor(inputs)
    normed = (inputs * scale_one * gain_one).astype(jnp.bfloat16)
    queries = jnp.dot(normed, w_query, preferred_element_type=jnp.float32)
    key_rows = jnp.dot(normed, w_key, preferred_element_type=jnp.float32)
    values = jnp.dot(normed, w_value, preferred_element_type=jnp.float32).astype(jnp.bfloat16)
    query_feats = make_features(queries).astype(jnp.bfloat16)
    key_feats = make_features(key_rows).astype(jnp.bfloat16)
    value_heads = values.reshape(token_count, -1, VD)
    heads_here = value_heads.shape[1]
    seg_blocks = segments.reshape(block_count, BLOCK)
    query_blocks = blocked(query_feats)
    key_blocks = blocked(key_feats)
    value_blocks = blocked(value_heads)
    ones_extra = jnp.ones((block_count, BLOCK, heads_here), jnp.bfloat16)
    states, totals, markers = segment_states(
        key_blocks, value_blocks, ones_extra, seg_blocks, False
    )
    numerator, denominator = lax.map(
        forward_block, (query_blocks, key_blocks, value_blocks, seg_blocks, states, totals, markers)
    )
    numerator = numerator.reshape(token_count, heads_here * VD)
    denominator = denominator.reshape(token_count, heads_here)
    own_numer, own_denom = (
        lax.psum_scatter(numerator, "feat", scatter_dimension=1, tiled=True),
        lax.psum_scatter(denominator, "feat", scatter_dimension=1, tiled=True),
    )
    context_exact = own_numer.reshape(token_count, head_share, VD) / own_denom[:, :, None]
    context_low = context_exact.reshape(token_count, column_share).astype(jnp.bfloat16)
    out_rows = lax.dynamic_slice_in_dim(w_out, feat_index * column_share, column_share, 0)
    mixed_rows = jnp.dot(
        lax.all_gather(context_low, "feat", axis=1, tiled=True),
        w_out,
        preferred_element_type=jnp.float32,
    )
    residual = inputs + live_rows * mixed_rows
    scale_two = rms_factor(residual)
    normed_two = (residual * scale_two * gain_two).astype(jnp.bfloat16)
    gate_values = jnp.dot(normed_two, w_gate, preferred_element_type=jnp.float32)
    up_values = jnp.dot(normed_two, w_up, preferred_element_type=jnp.float32)
    gate_sigmoid = jax.nn.sigmoid(gate_values)
    activated = gate_values * gate_sigmoid
    inner_rows = (activated * up_values).astype(jnp.bfloat16)
    feed_rows = lax.psum(
        jnp.dot(inner_rows, w_down, preferred_element_type=jnp.float32).astype(jnp.bfloat16), "feat"
    ).astype(jnp.float32)
    output = (residual + live_rows * feed_rows).astype(jnp.bfloat16)
    grad_output = cotangent.astype(jnp.float32)
    grad_feed = (grad_output * live_rows).astype(jnp.bfloat16)
    grad_wdown = jnp.einsum("tf,td->fd", inner_rows, grad_feed, preferred_element_type=jnp.float32)
    grad_inner = jnp.dot(grad_feed, w_down.T, preferred_element_type=jnp.float32)
    grad_gate = (
        grad_inner * up_values * gate_sigmoid * (1.0 + gate_values * (1.0 - gate_sigmoid))
    ).astype(jnp.bfloat16)
    grad_upper = (grad_inner * activated).astype(jnp.bfloat16)
    grad_wgate = jnp.einsum("td,tf->df", normed_two, grad_gate, preferred_element_type=jnp.float32)
    grad_wup = jnp.einsum("td,tf->df", normed_two, grad_upper, preferred_element_type=jnp.float32)
    grad_normed_part = jnp.dot(grad_gate, w_gate.T, preferred_element_type=jnp.float32) + jnp.dot(
        grad_upper, w_up.T, preferred_element_type=jnp.float32
    )
    grad_normed_two = lax.psum(grad_normed_part.astype(jnp.bfloat16), "feat").astype(jnp.float32)
    grad_gain_second, grad_resid_norm = norm_back(residual, scale_two, gain_two, grad_normed_two)
    grad_residual = grad_output + grad_resid_norm
    grad_mixed = (live_rows * grad_residual).astype(jnp.bfloat16)
    grad_wout = jnp.einsum("tc,td->cd", context_low, grad_mixed, preferred_element_type=jnp.float32)
    grad_context = jnp.dot(grad_mixed, out_rows.T, preferred_element_type=jnp.float32).astype(
        jnp.bfloat16
    )
    grad_context_heads = grad_context.astype(jnp.float32).reshape(token_count, head_share, VD)
    grad_own_numer = grad_context_heads / own_denom[:, :, None]
    grad_own_denom = -jnp.sum(grad_context_heads * context_exact, axis=2) / own_denom
    grad_numer, grad_denom = (
        lax.all_gather(
            grad_own_numer.reshape(token_count, column_share).astype(jnp.bfloat16),
            "feat",
            axis=1,
            tiled=True,
        ).astype(jnp.float32),
        lax.all_gather(grad_own_denom.astype(jnp.bfloat16), "feat", axis=1, tiled=True).astype(
            grad_own_denom.dtype
        ),
    )
    grad_numer_blocks = blocked(grad_numer.reshape(token_count, heads_here, VD))
    grad_denom_blocks = blocked(grad_denom)
    later_states, later_totals, later_markers = segment_states(
        query_blocks, grad_numer_blocks, grad_denom_blocks, seg_blocks, True
    )
    grad_qfeat, grad_kfeat, grad_vpart = lax.map(
        backward_block,
        (
            query_blocks,
            key_blocks,
            value_blocks,
            seg_blocks,
            grad_numer_blocks,
            grad_denom_blocks,
            states,
            totals,
            markers,
            later_states,
            later_totals,
            later_markers,
        ),
    )
    _, query_pull = jax.vjp(make_features, queries)
    _, key_pull = jax.vjp(make_features, key_rows)
    grad_query_part = query_pull(grad_qfeat.reshape(token_count, heads_here, slice_width))[0]
    grad_key_part = key_pull(grad_kfeat.reshape(token_count, heads_here, slice_width))[0]
    grad_value_part = grad_vpart.reshape(token_count, heads_here * VD)
    summed_query, summed_key, summed_value = (
        lax.psum(grad_query_part.astype(jnp.bfloat16), "feat").astype(jnp.float32),
        lax.psum(grad_key_part.astype(jnp.bfloat16), "feat").astype(jnp.float32),
        lax.psum(grad_value_part.astype(jnp.bfloat16), "feat").astype(jnp.float32),
    )
    grad_queries = summed_query.astype(jnp.bfloat16)
    grad_keys = summed_key.astype(jnp.bfloat16)
    grad_values = summed_value.astype(jnp.bfloat16)
    grad_wquery = jnp.einsum("td,tk->dk", normed, grad_queries, preferred_element_type=jnp.float32)
    grad_wkey = jnp.einsum("td,tk->dk", normed, grad_keys, preferred_element_type=jnp.float32)
    grad_wvalue = jnp.einsum("td,tk->dk", normed, grad_values, preferred_element_type=jnp.float32)
    grad_normed = (
        jnp.dot(grad_queries, w_query.T, preferred_element_type=jnp.float32)
        + jnp.dot(grad_keys, w_key.T, preferred_element_type=jnp.float32)
        + jnp.dot(grad_values, w_value.T, preferred_element_type=jnp.float32)
    )
    grad_gain_first, grad_input_norm = norm_back(inputs, scale_one, gain_one, grad_normed)
    grad_input = (grad_residual + grad_input_norm).astype(jnp.bfloat16)
    summed_all = (
        lax.psum_scatter(
            grad_wquery.astype(jnp.bfloat16), "dp", scatter_dimension=0, tiled=True
        ).astype(jnp.float32),
        lax.psum_scatter(
            grad_wkey.astype(jnp.bfloat16), "dp", scatter_dimension=0, tiled=True
        ).astype(jnp.float32),
        lax.psum_scatter(
            grad_wvalue.astype(jnp.bfloat16), "dp", scatter_dimension=0, tiled=True
        ).astype(jnp.float32),
        lax.psum_scatter(
            grad_wout.astype(jnp.bfloat16), "dp", scatter_dimension=1, tiled=True
        ).astype(jnp.float32),
        lax.psum_scatter(
            grad_gain_first.astype(jnp.bfloat16), "dp", scatter_dimension=0, tiled=True
        ).astype(jnp.float32),
        lax.psum_scatter(
            grad_wgate.astype(jnp.bfloat16), "dp", scatter_dimension=0, tiled=True
        ).astype(jnp.float32),
        lax.psum_scatter(
            grad_wup.astype(jnp.bfloat16), "dp", scatter_dimension=0, tiled=True
        ).astype(jnp.float32),
        lax.psum_scatter(
            grad_wdown.astype(jnp.bfloat16), "dp", scatter_dimension=1, tiled=True
        ).astype(jnp.float32),
        lax.psum_scatter(
            grad_gain_second.astype(jnp.bfloat16), "dp", scatter_dimension=0, tiled=True
        ).astype(jnp.float32),
    )
    (
        sum_query,
        sum_key,
        sum_value,
        sum_out,
        sum_gain_first,
        sum_gate,
        sum_up,
        sum_down,
        sum_gain_second,
    ) = summed_all
    return (
        output,
        grad_input,
        sum_gain_first,
        sum_query,
        sum_key,
        sum_value,
        sum_out,
        sum_gain_second,
        sum_gate,
        sum_up,
        sum_down,
    )


def solution(mesh):
    in_specs = (
        P("dp", None),
        P(),
        P(),
        P(),
        P(),
        P(),
        P(),
        P(None, "feat"),
        P(None, "feat"),
        P("feat", None),
        P("dp", None),
        P("dp", None),
    )
    out_specs = (
        P("dp", None),
        P("dp", None),
        P("dp"),
        P("dp", None),
        P("dp", None),
        P("dp", None),
        P("feat", "dp"),
        P("dp"),
        P("dp", "feat"),
        P("dp", "feat"),
        P("feat", "dp"),
    )
    return jax.shard_map(local, mesh=mesh, in_specs=in_specs, out_specs=out_specs, check_vma=False)
```

profile of v0, /device:TPU:0, one launch (start us, length us, event | category | flops | bytes accessed | tf_op | source)
XLA Modules:
  0.0 863.3 jit_solution(11175286774580664384)
XLA Ops:
  32.4 4.1 copy-done.1
  44.4 14.1 %all-reduce = f32[512,16]{0,1:T(8,128)} all-reduce(f32[512,16]{0,1:T(8,128)} %fusion.55), channel_id=3, replica_groups=mesh['dp'=8,'feat'=4] {'feat'}, use_global_device_ids=true, to_apply=%region_5.6.clone | all-reduce | flops 8192 | bytes 65536
  59.2 15.9 %reduce-scatter.17.cloned.1.call-done = f32[512,256]{0,1:T(8,128)} async-done(((f32[512,1024]{0,1:T(8,128)}), f32[512,256]{0,1:T(8,128)}) %reduce-scatter.17.cloned.1.call-update) | async-done | bytes 524304 | tf_op jit(solution)/shard_map/reduce_scatter | solution.py:210
  78.2 15.9 %all-gather.4.cloned.1.call-done = bf16[512,1024]{0,1:T(8,128)(2,1)} async-done(((bf16[512,256]{0,1:T(8,128)(2,1)}), bf16[512,1024]{0,1:T(8,128)(2,1)}) %all-gather.4.cloned.1.call-update) | async-done | bytes 1048592 | tf_op jit(solution)/shard_map/all_gather | solution.py:217
  108.9 36.2 %all-reduce.8.cloned.1.call-done = bf16[512,1024]{1,0:T(8,128)(2,1)} async-done(((bf16[512,1024]{1,0:T(8,128)(2,1)}), bf16[512,1024]{1,0:T(8,128)(2,1)}) %all-reduce.8.cloned.1.call-update) | async-done | bytes 1048592 | tf_op jit(solution)/shard_map/psum | solution.py:246
  158.9 6.0 all-gather
  171.6 10.2 %fusion.35 = f32[16,64,512]{2,1,0:T(8,128)} fusion(bf16[512,16,64]{0,2,1:T(8,128)(2,1)} %bitcast.117, f32[16,512,512]{1,2,0:T(8,128)} %copy-done.1, pred[512,512]{0,1:T(8,128)(4,1)S(1)} %fusion.31), kind=kOutput, calls=%fused_computation.87 | convolution fusion | flops 557842432 | bytes 20185088 | tf_op jit(solution)/shard_map/while/body/eval_jaxpr/hij,ihc->jhc/dot_general | solution.py:42
  181.8 9.8 %fusion.33 = f32[16,64,512]{2,1,0:T(8,128)} fusion(bf16[512,16,64]{0,2,1:T(8,128)(2,1)S(1)} %bitcast.118, f32[16,512,512]{1,2,0:T(8,128)} %copy-done.1, pred[512,512]{0,1:T(8,128)(4,1)S(1)} %fusion.31), kind=kOutput, calls=%fused_computation.85 | convolution fusion | flops 541065216 | bytes 20185088 | tf_op jit(solution)/shard_map/while/body/eval_jaxpr/hij,ihc->jhc/dot_general | solution.py:42
  191.6 9.7 %fusion.32 = f32[16,64,512]{2,1,0:T(8,128)} fusion(f32[16,512,512]{1,2,0:T(8,128)} %copy-done.1, pred[512,512]{0,1:T(8,128)(4,1)S(1)} %fusion.31, bf16[512,16,64]{0,2,1:T(8,128)(2,1)S(1)} %bitcast.119), kind=kOutput, calls=%fused_computation.84 | convolution fusion | flops 542638080 | bytes 20185088 | tf_op jit(solution)/shard_map/while/body/eval_jaxpr/hij,ihc->jhc/dot_general | solution.py:42
  203.2 8.1 fusion.90
  211.3 11.0 %add_select_fusion = f32[16,512,512]{1,2,0:T(8,128)} fusion(f32[16,512,512]{1,2,0:T(8,128)} %fusion.90, bf16[512,16,64]{0,2,1:T(8,128)(2,1)S(1)} %bitcast.127, f32[16,512]{1,0:T(8,128)S(1)} %copy-done.37, pred[512,512]{0,1:T(8,128)(4,1)S(1)} %fusion.31, bf16[512,16,64]{0,2,1:T(8,128)(2,1)S(1)} %bitcast.122), kind=kOutput, calls=%fused_computation.1 | convolution fusion | flops 551026688 | bytes 35946496 | tf_op jit(solution)/shard_map/while/body/eval_jaxpr/ihc,jhc->hij/dot_general | solution.py:42
  222.4 9.0 %fusion.64 = f32[16,69,512]{2,1,0:T(8,128)} fusion(bf16[512,16,69]{0,2,1:T(8,128)(2,1)S(1)} %copy-done.13, f32[16,512,512]{1,2,0:T(8,128)} %add_select_fusion), kind=kOutput, calls=%fused_computation.138 | convolution fusion | flops 583008256 | bytes 20168704 | tf_op jit(solution)/shard_map/while/body/eval_jaxpr/hij,jhf->ihf/dot_general | solution.py:42
  236.7 9.9 %fusion.62 = f32[16,69,512]{2,1,0:T(8,128)} fusion(bf16[512,16,69]{0,2,1:T(8,128)(2,1)S(1)} %get-tuple-element.138, f32[16,512,512]{1,2,0:T(8,128)} %add_select_fusion), kind=kOutput, calls=%fused_computation.136 | convolution fusion | flops 583008256 | bytes 20168704 | tf_op jit(solution)/shard_map/while/body/eval_jaxpr/hij,ihf->jhf/dot_general | solution.py:42
  246.6 14.8 %fusion.66 = f32[16,69,512]{2,1,0:T(8,128)} fusion(bf16[512,16,69]{0,2,1:T(8,128)(2,1)S(1)} %get-tuple-element.138, f32[16,512,512]{1,2,0:T(8,128)} %add_select_fusion), kind=kOutput, calls=%fused_computation.140 | convolution fusion | flops 595591168 | bytes 20168704 | tf_op jit(solution)/shard_map/while/body/eval_jaxpr/hij,ihf->jhf/dot_general | solution.py:42
  263.6 4.8 broadcast.180.clone
  268.4 11.4 %dynamic_update_slice.34 = f32[512,16,276]{0,2,1:T(8,128)} dynamic-update-slice(f32[512,16,276]{0,2,1:T(8,128)} %broadcast.180.clone, f32[512,16,69]{0,2,1:T(8,128)} %fusion.13, s32[]{:T(128)} %constant.119.clone.1, s32[]{:T(128)} %constant.119.clone.1, s32[]{:T(128)S(6)} %select_n.30) | dynamic-update-slice | bytes 4521988 | tf_op jit(solution)/shard_map/transpose(jvp())/dynamic_update_slice | solution.py:58
  279.8 4.8 slice_multiply_fusion.1
  285.9 5.7 multiply_reduce_fusion.2
  293.6 4.7 broadcast.180.clone.1
  298.3 11.4 %dynamic_update_slice.35 = f32[512,16,276]{0,2,1:T(8,128)} dynamic-update-slice(f32[512,16,276]{0,2,1:T(8,128)} %broadcast.180.clone.1, f32[512,16,69]{0,2,1:T(8,128)} %add_bitcast_fusion, s32[]{:T(128)} %constant.119.clone.1, s32[]{:T(128)} %constant.119.clone.1, s32[]{:T(128)S(6)} %select_n.30) | dynamic-update-slice | bytes 4521988 | tf_op jit(solution)/shard_map/transpose(jvp())/dynamic_update_slice | solution.py:58
  309.7 4.8 slice_multiply_fusion
  315.9 5.5 multiply_reduce_fusion
  345.0 42.0 %all-reduce.10.cloned.1.call-done = (bf16[512,1024]{1,0:T(8,128)(2,1)}, bf16[512,1024]{0,1:T(8,128)(2,1)}, bf16[512,256]{0,1:T(8,128)(2,1)}, bf16[512,256]{0,1:T(8,128)(2,1)}) async-done(((bf16[512,1024]{1,0:T(8,128)(2,1)}, bf16[512,1024]{0,1:T(8,128)(2,1)}, bf16[512,256]{0,1:T(8,128)(2,1)}, bf16[512,256]{0,1:T(8,128)(2,1)}), (bf16[512,1024]{1,0:T(8,128)(2,1)}, bf16[512,1024]{0,1:T(8,128)(2,1)}, ...) | async-done | bytes 2621456 | tf_op jit(solution)/shard_map/psum | solution.py:229
  397.0 55.2 %reduce-scatter.25.cloned.1.call-done = bf16[128,256]{1,0:T(8,128)(2,1)} async-done(((bf16[1024,256]{1,0:T(8,128)(2,1)}), bf16[128,256]{1,0:T(8,128)(2,1)}) %reduce-scatter.25.cloned.1.call-update) | async-done | bytes 65552
  453.8 66.0 %reduce-scatter.27.cloned.1.call-done = bf16[128,688]{1,0:T(8,128)(2,1)} async-done(((bf16[1024,688]{1,0:T(8,128)(2,1)}), bf16[128,688]{1,0:T(8,128)(2,1)}) %reduce-scatter.27.cloned.1.call-update) | async-done | bytes 176144
  521.7 65.4 %reduce-scatter.29.cloned.1.call-done = bf16[128,688]{1,0:T(8,128)(2,1)} async-done(((bf16[1024,688]{1,0:T(8,128)(2,1)}), bf16[128,688]{1,0:T(8,128)(2,1)}) %reduce-scatter.29.cloned.1.call-update) | async-done | bytes 176144
  589.0 65.8 %reduce-scatter.31.cloned.1.call-done = bf16[128,688]{1,0:T(8,128)(2,1)} async-done(((bf16[1024,688]{1,0:T(8,128)(2,1)}), bf16[128,688]{1,0:T(8,128)(2,1)}) %reduce-scatter.31.cloned.1.call-update) | async-done | bytes 176144
  661.9 19.3 %all-reduce.3 = (bf16[1024]{0:T(1024)(128)(2,1)S(1)}, bf16[1024]{0:T(1024)(128)(2,1)S(1)}) all-reduce(bf16[1024]{0:T(1024)(128)(2,1)S(1)} %get-tuple-element.111, bf16[1024]{0:T(1024)(128)(2,1)S(1)} %copy-done.48), channel_id=4, replica_groups=mesh['dp'=8,'feat'=4] {'dp'}, use_global_device_ids=true, to_apply=%region_20.21.clone | all-reduce | flops 2048 | bytes 8192
  681.9 5.3 fusion.19
  687.2 32.2 %reduce-scatter.19.cloned.1.call-done = bf16[128,256]{1,0:T(8,128)(2,1)} async-done(((bf16[1024,256]{1,0:T(8,128)(2,1)}), bf16[128,256]{1,0:T(8,128)(2,1)}) %reduce-scatter.19.cloned.1.call-update) | async-done | bytes 65552 | tf_op jit(solution)/shard_map/reduce_scatter | solution.py:314
  720.9 63.2 %reduce-scatter.21.cloned.1.call-done = bf16[128,256]{1,0:T(8,128)(2,1)} async-done(((bf16[1024,256]{1,0:T(8,128)(2,1)}), bf16[128,256]{1,0:T(8,128)(2,1)}) %reduce-scatter.21.cloned.1.call-update) | async-done | bytes 65552 | tf_op jit(solution)/shard_map/reduce_scatter | solution.py:317
  785.6 68.6 %reduce-scatter.23.cloned.1.call-done = bf16[128,1024]{1,0:T(8,128)(2,1)} async-done(((bf16[1024,1024]{1,0:T(8,128)(2,1)}), bf16[128,1024]{1,0:T(8,128)(2,1)}) %reduce-scatter.23.cloned.1.call-update) | async-done | bytes 262160 | tf_op jit(solution)/shard_map/reduce_scatter | solution.py:320
  (224 shorter events, 135.9 us)
Async XLA Ops:
  7.2 67.9 %reduce-scatter.17.cloned.1.call-start = ((), (), s32[]{:S(2)}) async-start(), calls=%async_computation.8 | async-start | bytes 2621440 | tf_op jit(solution)/shard_map/reduce_scatter | solution.py:210
  9.1 12.8 %copy-start.44 = (f32[512]{0:T(512)}, f32[512]{0:T(512)S(1)}, u32[]{:S(2)}) copy-start(f32[512]{0:T(512)S(1)} %add_rsqrt_fusion.1) | copy-start | bytes 6148
  15.1 6.7 copy-start.49
  40.8 36.2 %copy-start.50 = (s32[4]{0:T(128)S(1)}, s32[4]{0:T(128)}, u32[]{:S(2)}) copy-start(s32[4]{0:T(128)} %copy-done.49) | copy-start | bytes 52
  40.9 53.2 %all-gather.4.cloned.1.call-start = ((), (), s32[]{:S(2)}) async-start(), calls=%async_computation.9 | async-start | bytes 1310720 | tf_op jit(solution)/shard_map/all_gather | solution.py:217
  76.9 68.2 %all-reduce.8.cloned.1.call-start = ((), (), s32[]{:S(2)}) async-start(), calls=%async_computation.10 | async-start | bytes 2097152 | tf_op jit(solution)/shard_map/psum | solution.py:246
  108.8 62.7 %all-gather.6.cloned.1.call-start = ((), (), s32[]{:S(2)}) async-start(), calls=%async_computation.11 | async-start | bytes 1310720 | tf_op jit(solution)/shard_map/all_gather | solution.py:258
  154.3 232.7 %all-reduce.10.cloned.1.call-start = ((), (), s32[]{:S(2)}) async-start(), calls=%async_computation.19 | async-start | bytes 5242880 | tf_op jit(solution)/shard_map/psum | solution.py:229
  171.6 10.2 %copy-start.7 = (bf16[512,1024]{0,1:T(8,128)(2,1)S(1)}, bf16[512,1024]{0,1:T(8,128)(2,1)}, u32[]{:S(2)}) copy-start(bf16[512,1024]{0,1:T(8,128)(2,1)} %all-gather.6.cloned.1.call-done) | copy-start | bytes 3145732
  203.2 8.1 copy-start.37
  211.3 11.0 %copy-start.13 = (bf16[512,16,69]{0,2,1:T(8,128)(2,1)S(1)}, bf16[512,16,69]{0,2,1:T(8,128)(2,1)}, u32[]{:S(2)}) copy-start(bf16[512,16,69]{0,2,1:T(8,128)(2,1)} %copy-done.12) | copy-start | bytes 3391492
  222.4 11.4 %copy-start.2 = (f32[16,512,512]{1,2,0:T(8,128)S(1)}, f32[16,512,512]{1,2,0:T(8,128)}, u32[]{:S(2)}) copy-start(f32[16,512,512]{1,2,0:T(8,128)} %add_select_fusion) | copy-start | bytes 50331652
  246.6 14.8 %copy-start.20 = (f32[16,69,512]{2,1,0:T(8,128)S(1)}, f32[16,69,512]{2,1,0:T(8,128)}, u32[]{:S(2)}) copy-start(f32[16,69,512]{2,1,0:T(8,128)} %fusion.64) | copy-start | bytes 6782980
  246.6 14.8 %copy-start.21 = (f32[16,69,512]{2,1,0:T(8,128)S(1)}, f32[16,69,512]{2,1,0:T(8,128)}, u32[]{:S(2)}) copy-start(f32[16,69,512]{2,1,0:T(8,128)} %fusion.67) | copy-start | bytes 6782980
  246.6 14.8 %copy-start.22 = (f32[16,69,512]{2,1,0:T(8,128)S(1)}, f32[16,69,512]{2,1,0:T(8,128)}, u32[]{:S(2)}) copy-start(f32[16,69,512]{2,1,0:T(8,128)} %fusion.37) | copy-start | bytes 6782980
  246.6 14.8 %copy-start.41 = (f32[512,16]{0,1:T(8,128)S(1)}, f32[512,16]{0,1:T(8,128)}, u32[]{:S(2)}) copy-start(f32[512,16]{0,1:T(8,128)} %multiply_bitcast_fusion) | copy-start | bytes 98308
  279.8 6.1 copy-start.4
  279.8 6.1 copy-start.29
  309.7 6.1 copy-start.3
  309.7 6.1 copy-start.27
  315.9 8.7 %copy-start.24 = (f32[16,64,512]{2,1,0:T(8,128)S(1)}, f32[16,64,512]{2,1,0:T(8,128)}, u32[]{:S(2)}) copy-start(f32[16,64,512]{2,1,0:T(8,128)} %fusion.33) | copy-start | bytes 6291460
  315.9 8.7 %copy-start.25 = (f32[16,64,512]{2,1,0:T(8,128)S(1)}, f32[16,64,512]{2,1,0:T(8,128)}, u32[]{:S(2)}) copy-start(f32[16,64,512]{2,1,0:T(8,128)} %fusion.32) | copy-start | bytes 6291460
  326.3 125.9 %reduce-scatter.25.cloned.1.call-start = ((), (), s32[]{:S(2)}) async-start(), calls=%async_computation.15 | async-start | bytes 589824
  330.4 189.5 %reduce-scatter.27.cloned.1.call-start = ((), (), s32[]{:S(2)}) async-start(), calls=%async_computation.16 | async-start | bytes 1769472
  334.4 252.7 %reduce-scatter.29.cloned.1.call-start = ((), (), s32[]{:S(2)}) async-start(), calls=%async_computation.17 | async-start | bytes 1769472
  338.4 316.4 %reduce-scatter.31.cloned.1.call-start = ((), (), s32[]{:S(2)}) async-start(), calls=%async_computation.18 | async-start | bytes 1769472
  342.3 44.8 %copy-start.17 = (bf16[512,1024]{1,0:T(8,128)(2,1)S(1)}, bf16[512,1024]{1,0:T(8,128)(2,1)}, u32[]{:S(2)}) copy-start(bf16[512,1024]{1,0:T(8,128)(2,1)} %param.12) | copy-start | bytes 3145732
  342.3 44.8 %copy-start.45 = (f32[512]{0:T(512)S(1)}, f32[512]{0:T(512)}, u32[]{:S(2)}) copy-start(f32[512]{0:T(512)} %copy-done.44) | copy-start | bytes 6148
  342.3 44.8 %copy-start.47 = (f32[1024]{0:T(1024)S(1)}, f32[1024]{0:T(1024)}, u32[]{:S(2)}) copy-start(f32[1024]{0:T(1024)} %param.13) | copy-start | bytes 12292
  345.0 374.4 %reduce-scatter.19.cloned.1.call-start = ((), (), s32[]{:S(2)}) async-start(), calls=%async_computation.12 | async-start | bytes 589824 | tf_op jit(solution)/shard_map/reduce_scatter | solution.py:314
  389.5 394.6 %reduce-scatter.21.cloned.1.call-start = ((), (), s32[]{:S(2)}) async-start(), calls=%async_computation.13 | async-start | bytes 589824 | tf_op jit(solution)/shard_map/reduce_scatter | solution.py:317
  391.0 463.2 %reduce-scatter.23.cloned.1.call-start = ((), (), s32[]{:S(2)}) async-start(), calls=%async_computation.14 | async-start | bytes 2359296 | tf_op jit(solution)/shard_map/reduce_scatter | solution.py:320
  (40 other events, 98.8 us)
Sparse Core Ops, SparseCore 0:
  41.0 34.0 reduce-scatter.16
  77.3 16.7 all-gather.3
  109.0 36.1 all-reduce.7
  154.4 17.0 all-gather.5
  326.5 60.5 all-reduce.9
  390.2 61.9 reduce-scatter.24
  456.0 63.7 reduce-scatter.26
  523.3 63.8 reduce-scatter.28
  590.9 63.8 reduce-scatter.30
  658.6 60.7 reduce-scatter.18
  723.1 60.9 reduce-scatter.20
  787.5 66.7 reduce-scatter.22
where the time goes:
time: 875 us; the launch traced here: 863 us
  waiting for transfers between devices  531 us (61%)
  matrix products  151 us (17%)
  local copies, waits for them, and re-layouts  67.8 us (8%)
  other arithmetic  57.4 us (7%)
  blocking collectives  39.5 us (5%)
  between operations  16.5 us (2%)
    unnamed x16, waiting for transfers between devices  253 us
    dot_general x17, matrix products, exact_einsum(): jnp.einsum(form, left_part, right_part, preferred_element_type=jnp.float32)  99.6 us
    reduce_scatter x1, waiting for transfers between devices, local(): lax.psum_scatter(grad_wvalue.astype(jnp.bfloat16), 'dp', scatter_dimensio...  68.6 us
    reduce_scatter x1, waiting for transfers between devices, local(): lax.psum_scatter(grad_wkey.astype(jnp.bfloat16), 'dp', scatter_dimension=...  63.2 us
    psum x1, waiting for transfers between devices, local(): lax.psum(jnp.dot(inner_rows, w_down, preferred_element_type=jnp.float32)....  42 us
    psum x1, waiting for transfers between devices, local(): lax.psum(grad_normed_part.astype(jnp.bfloat16), 'feat').astype(jnp.float32)  36.2 us
    unnamed x2, blocking collectives  33.4 us
    reduce_scatter x1, waiting for transfers between devices, local(): lax.psum_scatter(grad_wquery.astype(jnp.bfloat16), 'dp', scatter_dimensio...  32.2 us
  transfers between devices with their start and end apart: 12, of which 12 were waited for; matrix products, arithmetic and copies ran while one was open for 7% of the time, Pallas kernels for 0%

commit v1 on v0

--- a/solution.py
+++ b/solution.py
@@ -243,7 +243,9 @@
     grad_normed_part = jnp.dot(grad_gate, w_gate.T, preferred_element_type=jnp.float32) + jnp.dot(
         grad_upper, w_up.T, preferred_element_type=jnp.float32
     )
-    grad_normed_two = lax.psum(grad_normed_part.astype(jnp.bfloat16), "feat").astype(jnp.float32)
+    grad_normed_two = jnp.sum(
+        lax.all_gather(grad_normed_part.astype(jnp.bfloat16), "feat"), axis=0
+    ).astype(jnp.float32)
     grad_gain_second, grad_resid_norm = norm_back(residual, scale_two, gain_two, grad_normed_two)
     grad_residual = grad_output + grad_resid_norm
     grad_mixed = (live_rows * grad_residual).astype(jnp.bfloat16)

time: 875 us -> 878 us (level)
    psum x1 -> x0, waiting for transfers between devices: 36.2 us -> none  [local(): lax.psum(grad_normed_part.astype(jnp.bfloat16), 'feat').astype(jnp.float32)]
    all_gather x0 -> x1, waiting for transfers between devices: none -> 34.6 us  [local(): lax.all_gather(grad_normed_part.astype(jnp.bfloat16), 'feat')]
    unnamed x131 -> x135, local copies, waits for them, and re-layouts: 31 us -> 31.1 us
where the time goes in v1:
time: 878 us; the launch traced here: 866 us
  waiting for transfers between devices  528 us (60%)
  matrix products  152 us (17%)
  local copies, waits for them, and re-layouts  67.9 us (8%)
  other arithmetic  61.8 us (7%)
  blocking collectives  39.6 us (5%)
  between operations  16.5 us (2%)
    unnamed x16, waiting for transfers between devices  252 us
    dot_general x17, matrix products, exact_einsum(): jnp.einsum(form, left_part, right_part, preferred_element_type=jnp.float32)  99.6 us
    reduce_scatter x1, waiting for transfers between devices, local(): lax.psum_scatter(grad_wvalue.astype(jnp.bfloat16), 'dp', scatter_dimensio...  69.1 us
    reduce_scatter x1, waiting for transfers between devices, local(): lax.psum_scatter(grad_wkey.astype(jnp.bfloat16), 'dp', scatter_dimension=...  62.7 us
    psum x1, waiting for transfers between devices, local(): lax.psum(jnp.dot(inner_rows, w_down, preferred_element_type=jnp.float32)....  40.9 us
    all_gather x1, waiting for transfers between devices, local(): lax.all_gather(grad_normed_part.astype(jnp.bfloat16), 'feat')  34.6 us
    unnamed x2, blocking collectives  33.6 us
    reduce_scatter x1, waiting for transfers between devices, local(): lax.psum_scatter(grad_wquery.astype(jnp.bfloat16), 'dp', scatter_dimensio...  32.8 us
  transfers between devices with their start and end apart: 12, of which 12 were waited for; matrix products, arithmetic and copies ran while one was open for 7% of the time, Pallas kernels for 0%

profile of v1, /device:TPU:0, one launch (start us, length us, event | category | flops | bytes accessed | tf_op | source)
XLA Modules:
  0.0 866.0 jit_solution(1422163268915153997)
XLA Ops:
  44.4 14.1 %all-reduce = f32[512,16]{0,1:T(8,128)} all-reduce(f32[512,16]{0,1:T(8,128)} %fusion.55), channel_id=4, replica_groups=mesh['dp'=8,'feat'=4] {'feat'}, use_global_device_ids=true, to_apply=%region_5.6.clone | all-reduce | flops 8192 | bytes 65536
  59.2 15.9 %reduce-scatter.17.cloned.1.call-done = f32[512,256]{0,1:T(8,128)} async-done(((f32[512,1024]{0,1:T(8,128)}), f32[512,256]{0,1:T(8,128)}) %reduce-scatter.17.cloned.1.call-update) | async-done | bytes 524304 | tf_op jit(solution)/shard_map/reduce_scatter | solution.py:210
  78.2 15.9 %all-gather.6.cloned.1.call-done = bf16[512,1024]{0,1:T(8,128)(2,1)} async-done(((bf16[512,256]{0,1:T(8,128)(2,1)}), bf16[512,1024]{0,1:T(8,128)(2,1)}) %all-gather.6.cloned.1.call-update) | async-done | bytes 1048592 | tf_op jit(solution)/shard_map/all_gather | solution.py:217
  108.9 34.6 %all-gather.10.cloned.1.call-done = bf16[2048,1024]{1,0:T(8,128)(2,1)} async-done(((bf16[512,1024]{1,0:T(8,128)(2,1)}), bf16[2048,1024]{1,0:T(8,128)(2,1)}) %all-gather.10.cloned.1.call-update) | async-done | bytes 4194320 | tf_op jit(solution)/shard_map/all_gather | solution.py:247
  143.5 4.4 reduce_sum.160
  161.6 6.0 all-gather.1
  173.9 10.2 %fusion.35 = f32[16,64,512]{2,1,0:T(8,128)} fusion(bf16[512,16,64]{0,2,1:T(8,128)(2,1)} %bitcast.118, f32[16,512,512]{1,2,0:T(8,128)} %copy-done.1, pred[512,512]{0,1:T(8,128)(4,1)S(1)} %fusion.31), kind=kOutput, calls=%fused_computation.87 | convolution fusion | flops 557842432 | bytes 20185088 | tf_op jit(solution)/shard_map/while/body/eval_jaxpr/hij,ihc->jhc/dot_general | solution.py:42
  184.2 9.8 %fusion.33 = f32[16,64,512]{2,1,0:T(8,128)} fusion(bf16[512,16,64]{0,2,1:T(8,128)(2,1)S(1)} %bitcast.119, f32[16,512,512]{1,2,0:T(8,128)} %copy-done.1, pred[512,512]{0,1:T(8,128)(4,1)S(1)} %fusion.31), kind=kOutput, calls=%fused_computation.85 | convolution fusion | flops 541065216 | bytes 20185088 | tf_op jit(solution)/shard_map/while/body/eval_jaxpr/hij,ihc->jhc/dot_general | solution.py:42
  194.0 9.7 %fusion.32 = f32[16,64,512]{2,1,0:T(8,128)} fusion(f32[16,512,512]{1,2,0:T(8,128)} %copy-done.1, pred[512,512]{0,1:T(8,128)(4,1)S(1)} %fusion.31, bf16[512,16,64]{0,2,1:T(8,128)(2,1)S(1)} %bitcast.120), kind=kOutput, calls=%fused_computation.84 | convolution fusion | flops 542638080 | bytes 20185088 | tf_op jit(solution)/shard_map/while/body/eval_jaxpr/hij,ihc->jhc/dot_general | solution.py:42
  205.6 8.1 fusion.90
  213.7 11.0 %add_select_fusion = f32[16,512,512]{1,2,0:T(8,128)} fusion(f32[16,512,512]{1,2,0:T(8,128)} %fusion.90, bf16[512,16,64]{0,2,1:T(8,128)(2,1)S(1)} %bitcast.128, f32[16,512]{1,0:T(8,128)S(1)} %copy-done.37, pred[512,512]{0,1:T(8,128)(4,1)S(1)} %fusion.31, bf16[512,16,64]{0,2,1:T(8,128)(2,1)S(1)} %bitcast.123), kind=kOutput, calls=%fused_computation.1 | convolution fusion | flops 551026688 | bytes 35946496 | tf_op jit(solution)/shard_map/while/body/eval_jaxpr/ihc,jhc->hij/dot_general | solution.py:42
  224.8 9.0 %fusion.64 = f32[16,69,512]{2,1,0:T(8,128)} fusion(bf16[512,16,69]{0,2,1:T(8,128)(2,1)S(1)} %copy-done.13, f32[16,512,512]{1,2,0:T(8,128)} %add_select_fusion), kind=kOutput, calls=%fused_computation.138 | convolution fusion | flops 583008256 | bytes 20168704 | tf_op jit(solution)/shard_map/while/body/eval_jaxpr/hij,jhf->ihf/dot_general | solution.py:42
  239.1 9.8 %fusion.62 = f32[16,69,512]{2,1,0:T(8,128)} fusion(bf16[512,16,69]{0,2,1:T(8,128)(2,1)S(1)} %get-tuple-element.138, f32[16,512,512]{1,2,0:T(8,128)} %add_select_fusion), kind=kOutput, calls=%fused_computation.136 | convolution fusion | flops 583008256 | bytes 20168704 | tf_op jit(solution)/shard_map/while/body/eval_jaxpr/hij,ihf->jhf/dot_general | solution.py:42
  249.0 14.8 %fusion.66 = f32[16,69,512]{2,1,0:T(8,128)} fusion(bf16[512,16,69]{0,2,1:T(8,128)(2,1)S(1)} %get-tuple-element.138, f32[16,512,512]{1,2,0:T(8,128)} %add_select_fusion), kind=kOutput, calls=%fused_computation.140 | convolution fusion | flops 595591168 | bytes 20168704 | tf_op jit(solution)/shard_map/while/body/eval_jaxpr/hij,ihf->jhf/dot_general | solution.py:42
  266.0 4.7 broadcast.180.clone
  270.8 11.4 %dynamic_update_slice.34 = f32[512,16,276]{0,2,1:T(8,128)} dynamic-update-slice(f32[512,16,276]{0,2,1:T(8,128)} %broadcast.180.clone, f32[512,16,69]{0,2,1:T(8,128)} %fusion.13, s32[]{:T(128)} %constant.120.clone.1, s32[]{:T(128)} %constant.120.clone.1, s32[]{:T(128)S(6)} %select_n.30) | dynamic-update-slice | bytes 4521988 | tf_op jit(solution)/shard_map/transpose(jvp())/dynamic_update_slice | solution.py:58
  282.2 4.8 slice_multiply_fusion.1
  288.3 5.7 multiply_reduce_fusion.2
  295.9 4.7 broadcast.180.clone.1
  300.7 11.4 %dynamic_update_slice.35 = f32[512,16,276]{0,2,1:T(8,128)} dynamic-update-slice(f32[512,16,276]{0,2,1:T(8,128)} %broadcast.180.clone.1, f32[512,16,69]{0,2,1:T(8,128)} %add_bitcast_fusion, s32[]{:T(128)} %constant.120.clone.1, s32[]{:T(128)} %constant.120.clone.1, s32[]{:T(128)S(6)} %select_n.30) | dynamic-update-slice | bytes 4521988 | tf_op jit(solution)/shard_map/transpose(jvp())/dynamic_update_slice | solution.py:58
  312.1 4.8 slice_multiply_fusion
  318.2 5.5 multiply_reduce_fusion
  348.5 40.9 %all-reduce.7.cloned.1.call-done = (bf16[512,1024]{1,0:T(8,128)(2,1)}, bf16[512,1024]{0,1:T(8,128)(2,1)}, bf16[512,256]{0,1:T(8,128)(2,1)}, bf16[512,256]{0,1:T(8,128)(2,1)}) async-done(((bf16[512,1024]{1,0:T(8,128)(2,1)}, bf16[512,1024]{0,1:T(8,128)(2,1)}, bf16[512,256]{0,1:T(8,128)(2,1)}, bf16[512,256]{0,1:T(8,128)(2,1)}), (bf16[512,1024]{1,0:T(8,128)(2,1)}, bf16[512,1024]{0,1:T(8,128)(2,1)}, ...) | async-done | bytes 2621456 | tf_op jit(solution)/shard_map/psum | solution.py:229
  399.4 58.6 %reduce-scatter.27.cloned.1.call-done = bf16[128,688]{1,0:T(8,128)(2,1)} async-done(((bf16[1024,688]{1,0:T(8,128)(2,1)}), bf16[128,688]{1,0:T(8,128)(2,1)}) %reduce-scatter.27.cloned.1.call-update) | async-done | bytes 176144
  459.8 65.4 %reduce-scatter.29.cloned.1.call-done = bf16[128,688]{1,0:T(8,128)(2,1)} async-done(((bf16[1024,688]{1,0:T(8,128)(2,1)}), bf16[128,688]{1,0:T(8,128)(2,1)}) %reduce-scatter.29.cloned.1.call-update) | async-done | bytes 176144
  527.0 65.8 %reduce-scatter.31.cloned.1.call-done = bf16[128,688]{1,0:T(8,128)(2,1)} async-done(((bf16[1024,688]{1,0:T(8,128)(2,1)}), bf16[128,688]{1,0:T(8,128)(2,1)}) %reduce-scatter.31.cloned.1.call-update) | async-done | bytes 176144
  594.7 62.3 %reduce-scatter.25.cloned.1.call-done = bf16[128,256]{1,0:T(8,128)(2,1)} async-done(((bf16[1024,256]{1,0:T(8,128)(2,1)}), bf16[128,256]{1,0:T(8,128)(2,1)}) %reduce-scatter.25.cloned.1.call-update) | async-done | bytes 65552
  663.9 19.5 %all-reduce.3 = (bf16[1024]{0:T(1024)(128)(2,1)S(1)}, bf16[1024]{0:T(1024)(128)(2,1)S(1)}) all-reduce(bf16[1024]{0:T(1024)(128)(2,1)S(1)} %get-tuple-element.111, bf16[1024]{0:T(1024)(128)(2,1)S(1)} %copy-done.50), channel_id=5, replica_groups=mesh['dp'=8,'feat'=4] {'dp'}, use_global_device_ids=true, to_apply=%region_20.21.clone | all-reduce | flops 2048 | bytes 8192
  684.0 5.3 fusion.19
  689.3 32.8 %reduce-scatter.19.cloned.1.call-done = bf16[128,256]{1,0:T(8,128)(2,1)} async-done(((bf16[1024,256]{1,0:T(8,128)(2,1)}), bf16[128,256]{1,0:T(8,128)(2,1)}) %reduce-scatter.19.cloned.1.call-update) | async-done | bytes 65552 | tf_op jit(solution)/shard_map/reduce_scatter | solution.py:316
  723.6 62.7 %reduce-scatter.21.cloned.1.call-done = bf16[128,256]{1,0:T(8,128)(2,1)} async-done(((bf16[1024,256]{1,0:T(8,128)(2,1)}), bf16[128,256]{1,0:T(8,128)(2,1)}) %reduce-scatter.21.cloned.1.call-update) | async-done | bytes 65552 | tf_op jit(solution)/shard_map/reduce_scatter | solution.py:319
  787.8 69.1 %reduce-scatter.23.cloned.1.call-done = bf16[128,1024]{1,0:T(8,128)(2,1)} async-done(((bf16[1024,1024]{1,0:T(8,128)(2,1)}), bf16[128,1024]{1,0:T(8,128)(2,1)}) %reduce-scatter.23.cloned.1.call-update) | async-done | bytes 262160 | tf_op jit(solution)/shard_map/reduce_scatter | solution.py:322
  (229 shorter events, 140.6 us)
Async XLA Ops:
  7.2 67.9 %reduce-scatter.17.cloned.1.call-start = ((), (), s32[]{:S(2)}) async-start(), calls=%async_computation.8 | async-start | bytes 2621440 | tf_op jit(solution)/shard_map/reduce_scatter | solution.py:210
  9.1 12.8 %copy-start.46 = (f32[512]{0:T(512)}, f32[512]{0:T(512)S(1)}, u32[]{:S(2)}) copy-start(f32[512]{0:T(512)S(1)} %add_rsqrt_fusion.1) | copy-start | bytes 6148
  15.1 6.7 copy-start.51
  40.8 36.2 %copy-start.52 = (s32[4]{0:T(128)S(1)}, s32[4]{0:T(128)}, u32[]{:S(2)}) copy-start(s32[4]{0:T(128)} %copy-done.51) | copy-start | bytes 52
  40.8 53.3 %all-gather.6.cloned.1.call-start = ((), (), s32[]{:S(2)}) async-start(), calls=%async_computation.9 | async-start | bytes 1310720 | tf_op jit(solution)/shard_map/all_gather | solution.py:217
  77.0 66.5 %all-gather.10.cloned.1.call-start = ((), (), s32[]{:S(2)}) async-start(), calls=%async_computation.14 | async-start | bytes 5242880 | tf_op jit(solution)/shard_map/all_gather | solution.py:247
  108.8 65.1 %all-gather.8.cloned.1.call-start = ((), (), s32[]{:S(2)}) async-start(), calls=%async_computation.10 | async-start | bytes 1310720 | tf_op jit(solution)/shard_map/all_gather | solution.py:260
  157.1 232.3 %all-reduce.7.cloned.1.call-start = ((), (), s32[]{:S(2)}) async-start(), calls=%async_computation.19 | async-start | bytes 5242880 | tf_op jit(solution)/shard_map/psum | solution.py:229
  173.9 10.2 %copy-start.7 = (bf16[512,1024]{0,1:T(8,128)(2,1)S(1)}, bf16[512,1024]{0,1:T(8,128)(2,1)}, u32[]{:S(2)}) copy-start(bf16[512,1024]{0,1:T(8,128)(2,1)} %all-gather.8.cloned.1.call-done) | copy-start | bytes 3145732
  205.6 8.1 copy-start.37
  213.7 11.0 %copy-start.13 = (bf16[512,16,69]{0,2,1:T(8,128)(2,1)S(1)}, bf16[512,16,69]{0,2,1:T(8,128)(2,1)}, u32[]{:S(2)}) copy-start(bf16[512,16,69]{0,2,1:T(8,128)(2,1)} %copy-done.12) | copy-start | bytes 3391492
  224.8 11.4 %copy-start.2 = (f32[16,512,512]{1,2,0:T(8,128)S(1)}, f32[16,512,512]{1,2,0:T(8,128)}, u32[]{:S(2)}) copy-start(f32[16,512,512]{1,2,0:T(8,128)} %add_select_fusion) | copy-start | bytes 50331652
  249.0 14.8 %copy-start.20 = (f32[16,69,512]{2,1,0:T(8,128)S(1)}, f32[16,69,512]{2,1,0:T(8,128)}, u32[]{:S(2)}) copy-start(f32[16,69,512]{2,1,0:T(8,128)} %fusion.64) | copy-start | bytes 6782980
  249.0 14.8 %copy-start.21 = (f32[16,69,512]{2,1,0:T(8,128)S(1)}, f32[16,69,512]{2,1,0:T(8,128)}, u32[]{:S(2)}) copy-start(f32[16,69,512]{2,1,0:T(8,128)} %fusion.67) | copy-start | bytes 6782980
  249.0 14.8 %copy-start.22 = (f32[16,69,512]{2,1,0:T(8,128)S(1)}, f32[16,69,512]{2,1,0:T(8,128)}, u32[]{:S(2)}) copy-start(f32[16,69,512]{2,1,0:T(8,128)} %fusion.37) | copy-start | bytes 6782980
  249.0 14.8 %copy-start.41 = (f32[512,16]{0,1:T(8,128)S(1)}, f32[512,16]{0,1:T(8,128)}, u32[]{:S(2)}) copy-start(f32[512,16]{0,1:T(8,128)} %multiply_bitcast_fusion) | copy-start | bytes 98308
  282.2 6.1 copy-start.4
  282.2 6.1 copy-start.30
  312.1 6.1 copy-start.3
  312.1 6.1 copy-start.28
  318.2 8.7 %copy-start.25 = (f32[16,64,512]{2,1,0:T(8,128)S(1)}, f32[16,64,512]{2,1,0:T(8,128)}, u32[]{:S(2)}) copy-start(f32[16,64,512]{2,1,0:T(8,128)} %fusion.33) | copy-start | bytes 6291460
  318.2 8.7 %copy-start.26 = (f32[16,64,512]{2,1,0:T(8,128)S(1)}, f32[16,64,512]{2,1,0:T(8,128)}, u32[]{:S(2)}) copy-start(f32[16,64,512]{2,1,0:T(8,128)} %fusion.32) | copy-start | bytes 6291460
  328.7 129.3 %reduce-scatter.27.cloned.1.call-start = ((), (), s32[]{:S(2)}) async-start(), calls=%async_computation.16 | async-start | bytes 1769472
  332.7 192.5 %reduce-scatter.29.cloned.1.call-start = ((), (), s32[]{:S(2)}) async-start(), calls=%async_computation.17 | async-start | bytes 1769472
  336.7 256.1 %reduce-scatter.31.cloned.1.call-start = ((), (), s32[]{:S(2)}) async-start(), calls=%async_computation.18 | async-start | bytes 1769472
  343.2 46.1 %copy-start.17 = (bf16[512,1024]{1,0:T(8,128)(2,1)S(1)}, bf16[512,1024]{1,0:T(8,128)(2,1)}, u32[]{:S(2)}) copy-start(bf16[512,1024]{1,0:T(8,128)(2,1)} %param.12) | copy-start | bytes 3145732
  343.3 46.1 %copy-start.47 = (f32[512]{0:T(512)S(1)}, f32[512]{0:T(512)}, u32[]{:S(2)}) copy-start(f32[512]{0:T(512)} %copy-done.46) | copy-start | bytes 6148
  343.3 46.1 %copy-start.49 = (f32[1024]{0:T(1024)S(1)}, f32[1024]{0:T(1024)}, u32[]{:S(2)}) copy-start(f32[1024]{0:T(1024)} %param.13) | copy-start | bytes 12292
  343.3 313.7 %reduce-scatter.25.cloned.1.call-start = ((), (), s32[]{:S(2)}) async-start(), calls=%async_computation.15 | async-start | bytes 589824
  348.4 373.7 %reduce-scatter.19.cloned.1.call-start = ((), (), s32[]{:S(2)}) async-start(), calls=%async_computation.11 | async-start | bytes 589824 | tf_op jit(solution)/shard_map/reduce_scatter | solution.py:316
  391.9 394.4 %reduce-scatter.21.cloned.1.call-start = ((), (), s32[]{:S(2)}) async-start(), calls=%async_computation.12 | async-start | bytes 589824 | tf_op jit(solution)/shard_map/reduce_scatter | solution.py:319
  393.4 463.6 %reduce-scatter.23.cloned.1.call-start = ((), (), s32[]{:S(2)}) async-start(), calls=%async_computation.13 | async-start | bytes 2359296 | tf_op jit(solution)/shard_map/reduce_scatter | solution.py:322
  (42 other events, 107.2 us)
Sparse Core Ops, SparseCore 0:
  41.0 34.1 reduce-scatter.16
  77.3 16.7 all-gather.5
  109.0 34.4 all-gather.9
  157.2 16.7 all-gather.7
  328.8 60.5 all-reduce.6
  393.0 64.8 reduce-scatter.26
  461.4 63.7 reduce-scatter.28
  529.0 63.7 reduce-scatter.30
  596.1 60.7 reduce-scatter.24
  661.1 60.9 reduce-scatter.18
  725.4 60.8 reduce-scatter.20
  790.1 66.8 reduce-scatter.22
